TPU v7x, 32 devices: a whole 2x2x4 slice. The times are simulated.
32 devices in a mesh: ang: 8 (over y, x, core), kslab: 4 (over z).
Axes of the slice: x: 2, y: 2, z: 4, core: 2. Of those that a mesh axis runs over, the one named last changes fastest.
Arguments:
- amplitude: bfloat16 [256, 112, 8, 2048], P('ang', None, 'kslab'), may hold values from -6 to 6
- ps_form: bfloat16 [2048, 896], replicated, may hold values from -0.125 to 0.125
- kgrid: float32 [8], replicated, may hold values from 0.1 to 3
- l_atom: int32 [112], replicated, may hold values from 0 to 7
- l_ps: int32 [112], replicated, may hold values from 0 to 7
- sixj: float32 [4, 12, 8, 8], replicated, may hold values from -0.5 to 0.5
Outputs:
- kernel: float32 [112, 4, 8, 896], P('ang', 'kslab')
All inputs are finite; a program needn't handle non-finite values.
Results may differ from a plain program's by a relative error of at most 0.0003.
Values sent between devices are 32-bit elements; how exact they have to be, the bound alone decides.
A program may use at most 128 MiB of HBM per device.

v0:
```python
import jax
import jax.numpy as jnp
from jax import lax
from jax.sharding import PartitionSpec as P


def legendre_table(first_row, row_count, total_points, degrees):
    positions = (first_row + jnp.arange(row_count)).astype(jnp.float32)
    angles = jnp.pi * (positions + 0.5) / total_points
    grid_nodes = jnp.cos(angles)
    grid_weights = jnp.pi / total_points * jnp.sin(angles)
    series = [jnp.ones_like(grid_nodes), grid_nodes]
    for degree in range(1, degrees - 1):
        series.append(
            ((2 * degree + 1) * grid_nodes * series[-1] - degree * series[-2]) / (degree + 1)
        )
    return (grid_nodes, grid_weights[None, :] * jnp.stack(series[:degrees]))


def recouple(values, channel_first, j_first, j_count, l_atom, l_ps, sixj, kpoints):
    channel_count = values.shape[0]
    levels = jnp.arange(sixj.shape[2], dtype=jnp.int32)
    atom_levels = lax.dynamic_slice_in_dim(l_atom, channel_first, channel_count)
    onehot_atom = (atom_levels[:, None] == levels[None, :]).astype(jnp.float32)
    onehot_ps = (l_ps[:, None] == levels[None, :]).astype(jnp.float32)
    table = lax.dynamic_slice_in_dim(sixj, j_first, j_count, 0)
    coupling = jnp.einsum(
        "jlxy,ax,by->ajlb", table, onehot_atom, onehot_ps, precision=lax.Precision.HIGHEST
    )
    widened = jnp.repeat(coupling, kpoints, axis=3)
    return jnp.einsum("ajlc,alkc->ajkc", widened, values, precision=lax.Precision.HIGHEST)


def local(amplitude, ps_form, kgrid, l_atom, l_ps, sixj):
    grid_count, channels, slab_points, radial = amplitude.shape
    columns = ps_form.shape[1]
    kpoints = kgrid.shape[0]
    ps_channels = columns // kpoints
    degrees = sixj.shape[1]
    total_j = sixj.shape[0]
    ang_size = lax.axis_size("ang")
    slab_size = lax.axis_size("kslab")
    owned = channels // ang_size
    owned_first = lax.axis_index("ang") * owned
    j_local = total_j // slab_size
    j_first = lax.axis_index("kslab") * j_local
    grid_nodes, projector = legendre_table(
        lax.axis_index("ang") * grid_count, grid_count, grid_count * ang_size, degrees
    )
    krow = lax.dynamic_slice_in_dim(kgrid, lax.axis_index("kslab") * slab_points, slab_points)[
        None, :, None
    ]
    kcol = jnp.tile(kgrid, ps_channels)[None, None, :]
    qinverse = 1.0 / (
        1.0 + krow * krow + kcol * kcol - 2.0 * grid_nodes[:, None, None] * krow * kcol
    )
    intersection = jnp.dot(
        amplitude.reshape(-1, radial), ps_form, preferred_element_type=jnp.float32
    )
    intersection = intersection.reshape(
        grid_count, lax.axis_size("ang") * owned, slab_points, columns
    )
    integrand = intersection * qinverse[:, None]
    summed = lax.psum_scatter(
        jnp.einsum("lg,gakc->alkc", projector, integrand, precision=lax.Precision.HIGHEST),
        "ang",
        scatter_dimension=0,
        tiled=True,
    )
    return recouple(
        lax.all_gather(summed, "kslab", axis=2, tiled=True),
        owned_first,
        j_first,
        j_local,
        l_atom,
        l_ps,
        sixj,
        kpoints,
    )


def solution(mesh):
    in_specs = (P("ang", None, "kslab", None), P(), P(), P(), P(), P())
    out_specs = P("ang", "kslab", None, None)
    return jax.shard_map(local, mesh=mesh, in_specs=in_specs, out_specs=out_specs, check_vma=False)
```

profile of v0, /device:TPU:0, one launch (start us, length us, event | category | flops | bytes accessed | tf_op | source)
XLA Modules:
  0.0 346.9 jit_solution(6099827794772779668)
XLA Ops:
  6.5 0.1 multiply_cosine_fusion
  6.8 0.1 subtract_multiply_fusion
  7.0 0.7 multiply_add_fusion
  7.7 0.7 tile.2
  8.4 0.1 broadcast_in_dim_tile.3
  8.5 0.1 broadcast_multiply_fusion
  8.6 0.1 broadcast_add_fusion
  8.6 0.2 subtract_divide_fusion
  8.8 44.6 %fusion.4 = f32[32,112,2,896]{3,1,2,0:T(8,128)} fusion(bf16[32,112,2,2048]{3,2,1,0:T(2,128)(2,1)} %param.6, f32[32,2,896]{2,1,0:T(2,128)S(1)} %subtract_divide_fusion, bf16[2048,896]{1,0:T(8,128)(2,1)} %param.7), kind=kOutput, calls=%fused_computation.4 | convolution fusion | flops 26313097216 | bytes 58949632 | tf_op jit(solution)/shard_map/dot_general | solution.py:57
  53.5 25.0 %fusion.7 = f32[112,12,2,896]{3,1,2,0:T(8,128)S(1)} fusion(f32[32,112,2,896]{3,1,2,0:T(8,128)} %fusion.4, f32[12,32]{1,0:T(8,128)S(1)} %stack.2, f32[32]{0:T(128)S(1)} %get-tuple-element.11), kind=kOutput, calls=%fused_computation.5 | convolution fusion | flops 924844416 | bytes 35325568 | tf_op jit(solution)/shard_map/lg,gakc->alkc/dot_general | solution.py:65
  78.5 8.6 %copy.14 = f32[112,12,2,896]{3,2,1,0:T(2,128)} copy(f32[112,12,2,896]{3,1,2,0:T(8,128)S(1)} %fusion.7) | data formatting | bytes 19267584 | tf_op jit(solution)/shard_map/lg,gakc->alkc/transpose | solution.py:65
  87.1 0.6 dynamic-slice
  88.4 142.1 %all-reduce.3.cloned.1.call-done = f32[112,12,2,896]{3,2,1,0:T(2,128)} async-done(((f32[112,12,2,896]{3,2,1,0:T(2,128)}), f32[112,12,2,896]{3,2,1,0:T(2,128)}) %all-reduce.3.cloned.1.call-update) | async-done | bytes 9633808
  230.4 1.7 constant_dynamic-slice_fusion
  232.1 1.4 copy.15
  233.5 0.1 copy.16
  233.7 0.1 dynamic_slice.10
  233.7 0.2 convolution_bitcast_fusion
  233.9 0.3 fusion.16
  234.2 5.6 %broadcast_in_dim.4 = f32[14,12,112,8]{3,2,0,1:T(8,128)} broadcast(f32[14,12,112]{2,0,1:T(8,128)S(1)} %fusion.16), dimensions={0,1,2} | broadcast | bytes 677376 | tf_op jit(solution)/shard_map/broadcast_in_dim | solution.py:30
  239.8 7.5 %broadcast_in_dim.5 = f32[14,12,896]{2,0,1:T(8,128)S(1)} reshape(f32[14,12,112,8]{3,2,0,1:T(8,128)} %broadcast_in_dim.4) | data formatting | bytes 1204224 | tf_op jit(solution)/shard_map/broadcast_in_dim | solution.py:30
  247.3 88.8 %all-gather.2.cloned.1.call-done = f32[14,12,8,896]{3,0,1,2:T(8,128)} async-done(((f32[14,12,2,896]{3,0,1,2:T(8,128)}), f32[14,12,8,896]{3,0,1,2:T(8,128)}) %all-gather.2.cloned.1.call-update) | async-done | bytes 4816912 | tf_op jit(solution)/shard_map/all_gather | solution.py:71
  336.1 3.1 multiply_reduce_fusion
  339.2 0.9 copy.37
  (21 shorter events, 0.5 us)
Async XLA Ops:
  6.5 227.0 %copy-start = (f32[4,12,8,8]{1,3,2,0:T(8,128)S(1)}, f32[4,12,8,8]{1,3,2,0:T(8,128)}, u32[]{:S(2)}) copy-start(f32[4,12,8,8]{1,3,2,0:T(8,128)} %param.11) | copy-start | bytes 36868
  6.5 223.9 %all-reduce.3.cloned.1.call-start = ((), (), s32[]{:S(2)}) async-start(), calls=%async_computation.1 | async-start | bytes 19267584
  78.4 8.7 %copy-start.3 = (u32[32]{0:T(128)S(1)}, u32[32]{0:T(128)}, u32[]{:S(2)}) copy-start(u32[32]{0:T(128)} %constant.104) | copy-start | bytes 388
  87.0 146.6 %copy-start.2 = (s32[112]{0:T(128)S(1)}, s32[112]{0:T(128)}, u32[]{:S(2)}) copy-start(s32[112]{0:T(128)} %param.9) | copy-start | bytes 1348
  87.0 146.9 %copy-start.1 = (s32[112]{0:T(128)S(1)}, s32[112]{0:T(128)}, u32[]{:S(2)}) copy-start(s32[112]{0:T(128)} %param.10) | copy-start | bytes 1348
  87.1 249.0 %all-gather.2.cloned.1.call-start = ((), (), s32[]{:S(2)}) async-start(), calls=%async_computation | async-start | bytes 6881280 | tf_op jit(solution)/shard_map/all_gather | solution.py:71
Sparse Core Ops, SparseCore 0:
  87.2 143.1 all-reduce.2
  233.6 102.3 all-gather.1
where the time goes:
time: 347 us
  waiting for transfers between devices  231 us (67%)
  matrix products  70 us (20%)
  local copies, waits for them, and re-layouts  27.2 us (8%)
  between operations  14.2 us (4%)
  other arithmetic  4.62 us (1%)
    unnamed x3, waiting for transfers between devices  142 us
    all_gather x1, waiting for transfers between devices, local(): lax.all_gather(summed, 'kslab', axis=2, tiled=True)  88.8 us
    dot_general x1, matrix products, local(): jnp.dot(amplitude.reshape(-1, radial), ps_form, preferred_element_type=jn...  44.6 us
    dot_general x1, matrix products, local(): jnp.einsum('lg,gakc->alkc', projector, integrand, precision=lax.Precision...  25 us
    broadcast_in_dim x2, local copies, waits for them, and re-layouts, recouple(): widened = jnp.repeat(coupling, kpoints, axis=3)  13.1 us
    transpose x1, local copies, waits for them, and re-layouts, local(): jnp.einsum('lg,gakc->alkc', projector, integrand, precision=lax.Precision...  8.58 us
  transfers between devices with their start and end apart: 2, of which 2 were waited for; matrix products, arithmetic and copies ran while one was open for 4% of the time, Pallas kernels for 0%

commit v1 on v0

v1 whole, which is shorter than its diff:
```python
import functools

import jax
import jax.numpy as jnp
from jax import lax
from jax.experimental import pallas as pl
from jax.experimental.pallas import tpu as pltpu
from jax.sharding import PartitionSpec as P


def legendre_table(first_row, row_count, total_points, degrees):
    positions = (first_row + jnp.arange(row_count)).astype(jnp.float32)
    angles = jnp.pi * (positions + 0.5) / total_points
    grid_nodes = jnp.cos(angles)
    grid_weights = jnp.pi / total_points * jnp.sin(angles)
    series = [jnp.ones_like(grid_nodes), grid_nodes]
    for degree in range(1, degrees - 1):
        series.append(
            ((2 * degree + 1) * grid_nodes * series[-1] - degree * series[-2]) / (degree + 1)
        )
    return (grid_nodes, grid_weights[None, :] * jnp.stack(series[:degrees]))


def recouple(values, l_atom, l_ps, sixj, kpoints):
    levels = jnp.arange(sixj.shape[2], dtype=jnp.int32)
    onehot_atom = (l_atom[:, None] == levels[None, :]).astype(jnp.float32)
    onehot_ps = (l_ps[:, None] == levels[None, :]).astype(jnp.float32)
    coupling = jnp.einsum(
        "jlxy,ax,by->ajlb", sixj, onehot_atom, onehot_ps, precision=lax.Precision.HIGHEST
    )
    widened = jnp.repeat(coupling, kpoints, axis=3)
    return jnp.einsum("ajlc,alkc->ajkc", widened, values, precision=lax.Precision.HIGHEST)


def plain(amplitude, ps_form, kgrid, l_atom, l_ps, sixj):
    grid_count, channels, slab_points, radial = amplitude.shape
    columns = ps_form.shape[1]
    kpoints = kgrid.shape[0]
    ps_channels = columns // kpoints
    degrees = sixj.shape[1]
    ang_size = lax.axis_size("ang")
    owned = channels // ang_size
    grid_nodes, projector = legendre_table(
        lax.axis_index("ang") * grid_count, grid_count, grid_count * ang_size, degrees
    )
    krow = lax.dynamic_slice_in_dim(kgrid, lax.axis_index("kslab") * slab_points, slab_points)[
        None, :, None
    ]
    kcol = jnp.tile(kgrid, ps_channels)[None, None, :]
    qinverse = 1.0 / (
        1.0 + krow * krow + kcol * kcol - 2.0 * grid_nodes[:, None, None] * krow * kcol
    )
    intersection = jnp.dot(
        amplitude.reshape(-1, radial), ps_form, preferred_element_type=jnp.float32
    )
    intersection = intersection.reshape(
        grid_count, lax.axis_size("ang") * owned, slab_points, columns
    )
    integrand = intersection * qinverse[:, None]
    partial = jnp.einsum("lg,gakc->alkc", projector, integrand, precision=lax.Precision.HIGHEST)
    partial = recouple(partial, l_atom, l_ps, sixj, kpoints)
    summed = lax.psum_scatter(partial, "ang", scatter_dimension=0, tiled=True)
    return lax.all_to_all(summed, "kslab", split_axis=1, concat_axis=2, tiled=True)


LANES = 128


def column_chunks(columns):
    width = 2 * LANES
    return [(first, min(width, columns - first)) for first in range(0, columns, width)]


def weigh(acc, weights, levels, partial, first_atom, chunk, sizes):
    grid_count, owned, slab_points, total_j = sizes
    first, width = chunk
    group = owned * slab_points
    for atom in range(owned):
        level = levels[first_atom + atom]
        for tile in range(width // LANES):
            lanes = pl.ds(first + tile * LANES, LANES)
            points = [
                acc[tile, pl.ds(atom * slab_points + k, grid_count, stride=group), :]
                for k in range(slab_points)
            ]
            rows = []
            for j in range(total_j):
                for k in range(slab_points):
                    term = points[k] * weights[level, j * slab_points + k, :, lanes]
                    rows.append(jnp.sum(term, axis=0, keepdims=True))
            partial[atom, :, lanes] = jnp.concatenate(rows, axis=0)


def fetch(amplitude, slab, sems, slot, first_atom, owned):
    return [
        pltpu.make_async_copy(
            amplitude.at[:, pl.ds(first_atom, owned), :, pl.ds(piece * LANES, LANES)],
            slab.at[slot, piece],
            sems.at[slot, piece],
        )
        for piece in range(slab.shape[1])
    ]


def block_kernel(sizes, amplitude, ps_form, weights, levels, partial, slab, acc_a, acc_b, sems):
    grid_count, owned, slab_points, total_j = sizes
    pieces = slab.shape[1]
    rows = grid_count * owned * slab_points
    blocks = partial.shape[0] // owned
    chunks = column_chunks(ps_form.shape[1])
    accs = (acc_a, acc_b)
    for copy in fetch(amplitude, slab, sems, 0, 0, owned):
        copy.start()

    def step(block, carry):
        slot = lax.rem(block, 2)
        first_atom = block * owned
        for copy in fetch(amplitude, slab, sems, slot, first_atom, owned):
            copy.wait()

        @pl.when(block + 1 < blocks)
        def _():
            for copy in fetch(amplitude, slab, sems, 1 - slot, first_atom + owned, owned):
                copy.start()

        left = jnp.concatenate(
            [slab.at[slot, piece].reshape(rows, LANES)[...] for piece in range(pieces)], axis=1
        )
        mine = partial.at[pl.ds(first_atom, owned)]
        for number, (first, width) in enumerate(chunks):
            product = jnp.dot(
                left, ps_form[:, pl.ds(first, width)], preferred_element_type=jnp.float32
            )
            acc = accs[number % 2]
            for tile in range(width // LANES):
                acc[tile] = product[:, tile * LANES : (tile + 1) * LANES]
            if number:
                weigh(
                    accs[1 - number % 2], weights, levels, mine, first_atom, chunks[number - 1], sizes
                )
        weigh(
            accs[(len(chunks) - 1) % 2], weights, levels, mine, first_atom, chunks[-1], sizes
        )
        return carry

    lax.fori_loop(0, blocks, step, 0)


def point_weights(sixj, projector, l_ps, qinverse):
    level_count = sixj.shape[2]
    onehot_ps = (l_ps[:, None] == jnp.arange(level_count, dtype=jnp.int32)).astype(jnp.float32)
    points = jnp.einsum("jlxy,lg->xjgy", sixj, projector, precision=lax.Precision.HIGHEST)
    widened = jnp.repeat(onehot_ps, qinverse.shape[2] // l_ps.shape[0], axis=0)
    spread = jnp.einsum("xjgy,cy->xjgc", points, widened, precision=lax.Precision.HIGHEST)
    value = spread[:, :, None] * jnp.transpose(qinverse, (1, 0, 2))[None, None]
    return value.reshape(level_count, -1, *value.shape[3:])


def local(amplitude, ps_form, kgrid, l_atom, l_ps, sixj):
    if amplitude.shape[2] != 2 or amplitude.shape[2] * sixj.shape[0] != 8:
        return plain(amplitude, ps_form, kgrid, l_atom, l_ps, sixj)
    grid_count, channels, slab_points, radial = amplitude.shape
    columns = ps_form.shape[1]
    kpoints = kgrid.shape[0]
    ps_channels = columns // kpoints
    degrees = sixj.shape[1]
    ang_size = lax.axis_size("ang")
    owned = channels // ang_size
    grid_nodes, projector = legendre_table(
        lax.axis_index("ang") * grid_count, grid_count, grid_count * ang_size, degrees
    )
    krow = lax.dynamic_slice_in_dim(kgrid, lax.axis_index("kslab") * slab_points, slab_points)[
        None, :, None
    ]
    kcol = jnp.tile(kgrid, ps_channels)[None, None, :]
    qinverse = 1.0 / (
        1.0 + krow * krow + kcol * kcol - 2.0 * grid_nodes[:, None, None] * krow * kcol
    )
    total_j = sixj.shape[0]
    sizes = (grid_count, owned, slab_points, total_j)
    rows = grid_count * owned * slab_points
    pieces = radial // LANES
    partial = pl.pallas_call(
        functools.partial(block_kernel, sizes),
        out_shape=jax.ShapeDtypeStruct((channels, total_j * slab_points, columns), jnp.float32),
        in_specs=[
            pl.BlockSpec(memory_space=pl.ANY),
            pl.BlockSpec(memory_space=pltpu.VMEM),
            pl.BlockSpec(memory_space=pltpu.VMEM),
            pl.BlockSpec(memory_space=pltpu.SMEM),
        ],
        out_specs=pl.BlockSpec(memory_space=pltpu.VMEM),
        scratch_shapes=[
            pltpu.VMEM((2, pieces, grid_count, owned, slab_points, LANES), jnp.bfloat16),
            pltpu.VMEM((2, rows, LANES), jnp.float32),
            pltpu.VMEM((2, rows, LANES), jnp.float32),
            pltpu.SemaphoreType.DMA((2, pieces)),
        ],
        compiler_params=pltpu.CompilerParams(vmem_limit_bytes=56 << 20),
        name="block_kernel",
    )(amplitude, ps_form, point_weights(sixj, projector, l_ps, qinverse), l_atom)
    summed = lax.psum_scatter(partial, "ang", scatter_dimension=0, tiled=True)
    summed = summed.reshape(owned, total_j, slab_points, columns)
    return lax.all_to_all(summed, "kslab", split_axis=1, concat_axis=2, tiled=True)


def solution(mesh):
    in_specs = (P("ang", None, "kslab", None), P(), P(), P(), P(), P())
    out_specs = P("ang", "kslab", None, None)
    return jax.shard_map(local, mesh=mesh, in_specs=in_specs, out_specs=out_specs, check_vma=False)
```

time: 347 us -> 144 us (0.41)
  waiting for transfers between devices: 231 us -> 49.5 us
  matrix products: 70 us -> 3.46 us
  Pallas kernels: 0 us -> 50.4 us
  local copies, waits for them, and re-layouts: 27.2 us -> 4.62 us
  blocking collectives: 0 us -> 16.3 us
    unnamed x3 -> x1, waiting for transfers between devices: 142 us -> 0.02 us
    all_gather x1 -> x0, waiting for transfers between devices: 88.8 us -> none  [local(): lax.all_gather(summed, 'kslab', axis=2, tiled=True)]
    dot_general x3 -> x2, matrix products: 69.8 us -> 3.46 us  [the longest x1 3.2 us: point_weights(): jnp.einsum('xjgy,cy->xjgc', points, widened, precision=lax.Precision.HIGH...]
    pallas_call x0 -> x1, Pallas kernels: none -> 50.4 us  [local(): pl.pallas_call(functools.partial(block_kernel, sizes), out_shape=jax.Shap...]
    reduce_scatter x0 -> x1, waiting for transfers between devices: none -> 49.5 us  [local(): summed = lax.psum_scatter(partial, 'ang', scatter_dimension=0, tiled=True)]
    all_to_all x0 -> x1, blocking collectives: none -> 16.3 us  [local(): lax.all_to_all(summed, 'kslab', split_axis=1, concat_axis=2, tiled=True)]
    broadcast_in_dim x2 -> x1, local copies, waits for them, and re-layouts: 13.1 us -> 0.17 us  [point_weights(): widened = jnp.repeat(onehot_ps, qinverse.shape[2] // l_ps.shape[0], axis=0)]
    transpose x1 -> x0, local copies, waits for them, and re-layouts: 8.58 us -> none  [local(): jnp.einsum('lg,gakc->alkc', projector, integrand, precision=lax.Precision...]
  transfers between devices with their start and end apart: 2 -> 1, of which waited for: 2 -> 1; matrix products, arithmetic and copies ran while one was open for 4% -> 0% of each run, Pallas kernels for 0% -> 0%
where the time goes in v1:
time: 144 us
  Pallas kernels  50.4 us (35%)
  waiting for transfers between devices  49.5 us (34%)
  blocking collectives  16.3 us (11%)
  between operations  13.5 us (9%)
  other arithmetic  5.87 us (4%)
  local copies, waits for them, and re-layouts  4.62 us (3%)
  matrix products  3.46 us (2%)
    pallas_call x1, Pallas kernels, local(): pl.pallas_call(functools.partial(block_kernel, sizes), out_shape=jax.Shap...  50.4 us
    reduce_scatter x1, waiting for transfers between devices, local(): summed = lax.psum_scatter(partial, 'ang', scatter_dimension=0, tiled=True)  49.5 us
    all_to_all x1, blocking collectives, local(): lax.all_to_all(summed, 'kslab', split_axis=1, concat_axis=2, tiled=True)  16.3 us
    mul x1, other arithmetic, point_weights(): value = spread[:, :, None] * jnp.transpose(qinverse, (1, 0, 2))[None, None]  3.79 us
    dot_general x1, matrix products, point_weights(): jnp.einsum('xjgy,cy->xjgc', points, widened, precision=lax.Precision.HIGH...  3.2 us
  transfers between devices with their start and end apart: 1, of which 1 were waited for; matrix products, arithmetic and copies ran while one was open for 0% of the time, Pallas kernels for 0%

profile of v1, /device:TPU:0, one launch (start us, length us, event | category | flops | bytes accessed | tf_op | source)
XLA Modules:
  0.0 143.6 jit_solution(11402164722826505611)
XLA Ops:
  6.6 0.1 broadcast_multiply_fusion.7
  6.6 0.1 broadcast_multiply_fusion.3
  6.7 0.1 broadcast_multiply_fusion.5
  6.8 0.1 subtract_multiply_fusion
  6.9 0.1 multiply_cosine_fusion
  7.0 0.7 fusion.6
  7.7 0.7 multiply_add_fusion
  8.4 0.7 tile.2
  9.1 0.1 broadcast_in_dim_tile.3
  9.2 0.2 broadcast_in_dim.2
  9.3 0.2 reshape.285
  9.6 0.1 broadcast_multiply_fusion.1
  9.6 0.1 broadcast_add_fusion
  9.7 0.1 subtract_divide_fusion
  9.9 0.3 convolution_bitcast_fusion
  10.1 3.2 %fusion.1 = f32[8,4,32,896]{3,2,1,0:T(8,128)S(1)} fusion(f32[8,4,32,8]{2,3,1,0:T(8,128)S(1)} %convolution_bitcast_fusion, f32[896,8,1,1]{0,1,2,3:T(8,128)S(1)} %reshape.285), kind=kOutput, calls=%fused_computation.4 | convolution fusion | flops 88080384 | bytes 3731456 | tf_op jit(solution)/shard_map/xjgy,cy->xjgc/dot_general | solution.py:154
  13.4 0.1 mul.988
  13.4 1.0 mul.975
  14.4 3.8 %broadcast_multiply_fusion.weights = f32[8,8,32,896]{3,2,1,0:T(8,128)} fusion(f32[8,8,32,896]{3,2,1,0:T(8,128)S(1)} %bitcast.14, f32[8,32,896]{2,1,0:T(8,128)S(1)} %bitcast.15), kind=kLoop, calls=%fused_computation | loop fusion | flops 1835008 | bytes 15597568 | tf_op jit(solution)/shard_map/mul | solution.py:155
  18.2 50.4 %block_kernel.1 = f32[112,8,896]{2,1,0:T(8,128)} custom-call(bf16[32,112,2,2048]{3,2,1,0:T(2,128)(2,1)} %amplitude.1, bf16[2048,896]{1,0:T(8,128)(2,1)} %ps_form.1, f32[8,8,32,896]{3,2,1,0:T(8,128)} %broadcast_multiply_fusion.weights, s32[112]{0:T(128)} %levels.1), custom_call_target="tpu_custom_call" | custom-call | tf_op jit(solution)/shard_map/block_kernel/pallas_call | solution.py:183
  68.6 49.5 %reduce-scatter.2.cloned.1.call-done = f32[14,8,896]{2,1,0:T(8,128)} async-done(((f32[112,8,896]{2,1,0:T(8,128)}), f32[14,8,896]{2,1,0:T(8,128)}) %reduce-scatter.2.cloned.1.call-update) | async-done | bytes 401424 | tf_op jit(solution)/shard_map/reduce_scatter | solution.py:202
  118.1 1.2 reshape.283
  119.4 16.3 %all_to_all.12 = f32[14,4,2,896]{3,2,0,1:T(2,128)S(1)} all-to-all(f32[14,4,2,896]{3,2,0,1:T(2,128)S(1)} %copy.10), channel_id=1, replica_groups=mesh['ang'=8,'kslab'=4] {'kslab'}, dimensions={1} | all-to-all | bytes 802816 | tf_op jit(solution)/shard_map/all_to_all | solution.py:204
  135.7 1.0 all_to_all.10
  (11 shorter events, 0.3 us)
Async XLA Ops:
  6.5 3.4 %copy-start = (f32[4,12,8,8]{1,3,2,0:T(8,128)S(1)}, f32[4,12,8,8]{1,3,2,0:T(8,128)}, u32[]{:S(2)}) copy-start(f32[4,12,8,8]{1,3,2,0:T(8,128)} %param.11) | copy-start | bytes 36868
  6.5 111.5 %reduce-scatter.2.cloned.1.call-start = ((), (), s32[]{:S(2)}) async-start(), calls=%async_computation.2 | async-start | bytes 3612672 | tf_op jit(solution)/shard_map/reduce_scatter | solution.py:202
Sparse Core Ops, SparseCore 0:
  68.7 49.2 reduce-scatter.1

commit v2 on v1

--- a/solution.py
+++ b/solution.py
@@ -64,11 +64,12 @@
 
 
 LANES = 128
+HALVES = 2
 
 
 def column_chunks(columns):
-    width = 2 * LANES
-    return [(first, min(width, columns - first)) for first in range(0, columns, width)]
+    width = LANES * (-(-columns // (2 * LANES)))
+    return [(0, width), (width, columns - width)]
 
 
 def weigh(acc, weights, levels, partial, first_atom, chunk, sizes):
@@ -102,62 +103,250 @@
     ]
 
 
-def block_kernel(sizes, amplitude, ps_form, weights, levels, partial, slab, acc_a, acc_b, sems):
+def block_kernel(
+    sizes,
+    amplitude,
+    ps_source,
+    points,
+    ps_levels,
+    kgrid,
+    levels,
+    out,
+    ps_form,
+    onehot,
+    qinverse,
+    slab,
+    acc_a,
+    acc_b,
+    weights,
+    parts,
+    core_in,
+    chip_in,
+    slices,
+    slices_in,
+    sems,
+    core_sems,
+    chip_sems,
+    slab_sems,
+    ps_sem,
+):
     grid_count, owned, slab_points, total_j = sizes
     pieces = slab.shape[1]
     rows = grid_count * owned * slab_points
-    blocks = partial.shape[0] // owned
+    blocks = 2 * chip_in.shape[1] + 2
+    halves = parts.shape[0] // blocks
+    chips = blocks // 2
+    last_acc = (acc_a, acc_b)[1]
+    kpoints = kgrid.shape[0]
+    columns = ps_form.shape[1]
     chunks = column_chunks(ps_form.shape[1])
     accs = (acc_a, acc_b)
-    for copy in fetch(amplitude, slab, sems, 0, 0, owned):
+    me = lax.axis_index("ang")
+    z = lax.axis_index("kslab")
+    core = lax.rem(me, 2)
+    chip_x = lax.rem(me // 2, 2)
+    chip_y = me // 4
+    other_core = me + 1 - 2 * core
+
+    def chip_at(turn):
+        x = lax.rem(chip_x + 1 - turn // 2, 2)
+        y = lax.rem(chip_y + lax.rem(turn + 1, 2), 2)
+        return 2 * y + x
+
+    def first_of(unit):
+        half, block = unit // blocks, lax.rem(unit, blocks)
+        owner = 2 * chip_at(block // 2) + lax.rem(core + 1 + lax.rem(block, 2), 2)
+        return (owner * halves + half) * owned
+
+    def to_core(half, turn):
+        return pltpu.make_async_remote_copy(
+            src_ref=parts.at[half * blocks + 2 * turn],
+            dst_ref=core_in.at[half, turn],
+            send_sem=core_sems.at[0, half, turn],
+            recv_sem=core_sems.at[1, half, turn],
+            device_id={"ang": other_core},
+            device_id_type=pl.DeviceIdType.MESH,
+        )
+
+    def to_chip(half, turn):
+        return pltpu.make_async_remote_copy(
+            src_ref=parts.at[half * blocks + 2 * turn + 1],
+            dst_ref=chip_in.at[half, turn],
+            send_sem=chip_sems.at[0, half, turn],
+            recv_sem=chip_sems.at[1, half, turn],
+            device_id={"ang": 2 * chip_at(turn) + core},
+            device_id_type=pl.DeviceIdType.MESH,
+        )
+
+    def to_slab(half, away):
+        target = lax.rem(z + away, total_j)
+        return pltpu.make_async_remote_copy(
+            src_ref=slices.at[half, target],
+            dst_ref=slices_in.at[half, z],
+            send_sem=slab_sems.at[0, half, away],
+            recv_sem=slab_sems.at[1, half, away],
+            device_id={"kslab": target},
+            device_id_type=pl.DeviceIdType.MESH,
+        )
+
+    for copy in fetch(amplitude, slab, sems, 0, first_of(0), owned):
         copy.start()
-
-    def step(block, carry):
-        slot = lax.rem(block, 2)
-        first_atom = block * owned
-        for copy in fetch(amplitude, slab, sems, slot, first_atom, owned):
-            copy.wait()
-
-        @pl.when(block + 1 < blocks)
-        def _():
-            for copy in fetch(amplitude, slab, sems, 1 - slot, first_atom + owned, owned):
-                copy.start()
-
+    ps_copy = pltpu.make_async_copy(ps_source, ps_form, ps_sem)
+    ps_copy.start()
+    barrier = pltpu.get_barrier_semaphore()
+    greeted = [{"ang": other_core}]
+    greeted += [{"ang": 2 * chip_at(turn) + core} for turn in range(chips - 1)]
+    greeted += [{"kslab": lax.rem(z + away, total_j)} for away in range(1, total_j)]
+    for device in greeted:
+        pl.semaphore_signal(
+            barrier, inc=1, device_id=device, device_id_type=pl.DeviceIdType.MESH
+        )
+    pl.semaphore_wait(barrier, len(greeted))
+
+    member = lax.broadcasted_iota(jnp.int32, (ps_levels.shape[1], columns), 1) - (
+        kpoints * lax.broadcasted_iota(jnp.int32, (ps_levels.shape[1], columns), 0)
+    )
+    member = jnp.where((member >= 0) & (member < kpoints), 1.0, 0.0).astype(jnp.bfloat16)
+    level_rows = lax.broadcasted_iota(jnp.int32, (weights.shape[0], ps_levels.shape[1]), 0)
+    known = jnp.where(level_rows == ps_levels[...], 1.0, 0.0).astype(jnp.bfloat16)
+    onehot[...] = jnp.dot(known, member, preferred_element_type=jnp.float32)
+
+    tile_shape = (grid_count, LANES)
+    place = me * grid_count + lax.broadcasted_iota(jnp.int32, tile_shape, 0)
+    total_points = grid_count * blocks
+    nodes = jnp.cos(jnp.pi * (place.astype(jnp.float32) + 0.5) / total_points)
+    kindex = lax.broadcasted_iota(jnp.int32, tile_shape, 1) & (kpoints - 1)
+    kcol = jnp.zeros(tile_shape, jnp.float32)
+    for q in range(kpoints):
+        kcol = jnp.where(kindex == q, kgrid[q], kcol)
+    for k in range(slab_points):
+        krow = kgrid[z * slab_points + k]
+        value = 1.0 / (1.0 + krow * krow + kcol * kcol - 2.0 * nodes * krow * kcol)
+        for tile in range(columns // LANES):
+            qinverse[k, :, tile * LANES : (tile + 1) * LANES] = value
+
+    def weight_level(level, carry):
+        spread = jnp.dot(
+            points[level],
+            onehot[...],
+            precision=lax.Precision.HIGHEST,
+            preferred_element_type=jnp.float32,
+        )
+        for j in range(total_j):
+            for k in range(slab_points):
+                weights[level, j * slab_points + k] = (
+                    spread[j * grid_count : (j + 1) * grid_count] * qinverse[k]
+                )
+        return carry
+
+    lax.fori_loop(0, weights.shape[0], weight_level, 0)
+    last_acc[...] = jnp.zeros_like(last_acc)
+    ps_copy.wait()
+
+    def multiply(slot, number):
+        first, width = chunks[number]
         left = jnp.concatenate(
             [slab.at[slot, piece].reshape(rows, LANES)[...] for piece in range(pieces)], axis=1
         )
-        mine = partial.at[pl.ds(first_atom, owned)]
-        for number, (first, width) in enumerate(chunks):
-            product = jnp.dot(
-                left, ps_form[:, pl.ds(first, width)], preferred_element_type=jnp.float32
+        product = jnp.dot(
+            left, ps_form[:, pl.ds(first, width)], preferred_element_type=jnp.float32
+        )
+        for tile in range(width // LANES):
+            accs[number][tile] = product[:, tile * LANES : (tile + 1) * LANES]
+
+    def weigh_unit(unit, number):
+        weigh(
+            accs[number], weights, levels, parts.at[unit], first_of(unit), chunks[number], sizes
+        )
+
+    def finish(unit):
+        half, block = unit // blocks, lax.rem(unit, blocks)
+        turn = block // 2
+
+        @pl.when(lax.rem(block, 2) == 0)
+        def _():
+            to_core(half, turn).start()
+
+        @pl.when(lax.rem(block, 2) == 1)
+        def _():
+            to_core(half, turn).wait_recv()
+
+            @pl.when(turn < chips - 1)
+            def _():
+                parts[unit] = parts[unit] + core_in[half, turn]
+                to_chip(half, turn).start()
+
+            @pl.when(turn == chips - 1)
+            def _():
+                for earlier in range(chips - 1):
+                    to_chip(half, earlier).wait_recv()
+
+                def total_atom(atom, carry):
+                    total = parts[unit, atom] + core_in[half, chips - 1, atom]
+                    for earlier in range(chips - 1):
+                        total = total + chip_in[half, earlier, atom]
+                    for j in range(total_j):
+                        slices[half, j, atom] = total[j * slab_points : (j + 1) * slab_points]
+                    return carry
+
+                lax.fori_loop(0, owned, total_atom, 0)
+                for away in range(1, total_j):
+                    to_slab(half, away).start()
+                slices_in[half, z] = slices[half, z]
+
+    def step(unit, carry):
+        slot = lax.rem(unit, 2)
+        for copy in fetch(amplitude, slab, sems, slot, first_of(unit), owned):
+            copy.wait()
+
+        @pl.when(unit + 1 < halves * blocks)
+        def _():
+            for copy in fetch(amplitude, slab, sems, 1 - slot, first_of(unit + 1), owned):
+                copy.start()
+
+        multiply(slot, 0)
+        weigh_unit(jnp.maximum(unit - 1, 0), 1)
+
+        @pl.when(unit > 0)
+        def _():
+            finish(unit - 1)
+
+        multiply(slot, 1)
+        weigh_unit(unit, 0)
+        return carry
+
+    units = halves * blocks
+    lax.fori_loop(0, units, step, 0)
+    weigh_unit(units - 1, 1)
+    finish(units - 1)
+
+    for half in range(halves):
+        for away in range(1, total_j):
+            to_slab(half, away).wait_recv()
+
+        def place_atom(atom, carry):
+            out[half * owned + atom, 0] = jnp.concatenate(
+                [slices_in[half, j, atom] for j in range(total_j)], axis=0
             )
-            acc = accs[number % 2]
-            for tile in range(width // LANES):
-                acc[tile] = product[:, tile * LANES : (tile + 1) * LANES]
-            if number:
-                weigh(
-                    accs[1 - number % 2], weights, levels, mine, first_atom, chunks[number - 1], sizes
-                )
-        weigh(
-            accs[(len(chunks) - 1) % 2], weights, levels, mine, first_atom, chunks[-1], sizes
-        )
-        return carry
-
-    lax.fori_loop(0, blocks, step, 0)
-
-
-def point_weights(sixj, projector, l_ps, qinverse):
-    level_count = sixj.shape[2]
-    onehot_ps = (l_ps[:, None] == jnp.arange(level_count, dtype=jnp.int32)).astype(jnp.float32)
+            return carry
+
+        lax.fori_loop(0, owned, place_atom, 0)
+    for half in range(halves):
+        for turn in range(chips):
+            to_core(half, turn).wait_send()
+        for turn in range(chips - 1):
+            to_chip(half, turn).wait_send()
+        for away in range(1, total_j):
+            to_slab(half, away).wait_send()
+
+
+def point_weights(sixj, projector):
     points = jnp.einsum("jlxy,lg->xjgy", sixj, projector, precision=lax.Precision.HIGHEST)
-    widened = jnp.repeat(onehot_ps, qinverse.shape[2] // l_ps.shape[0], axis=0)
-    spread = jnp.einsum("xjgy,cy->xjgc", points, widened, precision=lax.Precision.HIGHEST)
-    value = spread[:, :, None] * jnp.transpose(qinverse, (1, 0, 2))[None, None]
-    return value.reshape(level_count, -1, *value.shape[3:])
+    return points.reshape(sixj.shape[2], -1, sixj.shape[3])
 
 
 def local(amplitude, ps_form, kgrid, l_atom, l_ps, sixj):
-    if amplitude.shape[2] != 2 or amplitude.shape[2] * sixj.shape[0] != 8:
+    if (amplitude.shape[2], sixj.shape[0], lax.axis_size("ang"), lax.axis_size("kslab")) != (2, 4, 8, 4):
         return plain(amplitude, ps_form, kgrid, l_atom, l_ps, sixj)
     grid_count, channels, slab_points, radial = amplitude.shape
     columns = ps_form.shape[1]
@@ -169,39 +358,56 @@
     grid_nodes, projector = legendre_table(
         lax.axis_index("ang") * grid_count, grid_count, grid_count * ang_size, degrees
     )
-    krow = lax.dynamic_slice_in_dim(kgrid, lax.axis_index("kslab") * slab_points, slab_points)[
-        None, :, None
-    ]
-    kcol = jnp.tile(kgrid, ps_channels)[None, None, :]
-    qinverse = 1.0 / (
-        1.0 + krow * krow + kcol * kcol - 2.0 * grid_nodes[:, None, None] * krow * kcol
-    )
     total_j = sixj.shape[0]
-    sizes = (grid_count, owned, slab_points, total_j)
-    rows = grid_count * owned * slab_points
+    halves = HALVES if owned % HALVES == 0 else 1
+    share = owned // halves
+    sizes = (grid_count, share, slab_points, total_j)
+    rows = grid_count * share * slab_points
+    wide = column_chunks(columns)
     pieces = radial // LANES
-    partial = pl.pallas_call(
+    level_count = sixj.shape[2]
+    parts_shape = (share, total_j * slab_points, columns)
+    slice_shape = (halves, total_j, share, slab_points, columns)
+    chips = ang_size // 2
+    in_vmem = pl.BlockSpec(memory_space=pltpu.VMEM)
+    return pl.pallas_call(
         functools.partial(block_kernel, sizes),
-        out_shape=jax.ShapeDtypeStruct((channels, total_j * slab_points, columns), jnp.float32),
-        in_specs=[
-            pl.BlockSpec(memory_space=pl.ANY),
-            pl.BlockSpec(memory_space=pltpu.VMEM),
-            pl.BlockSpec(memory_space=pltpu.VMEM),
-            pl.BlockSpec(memory_space=pltpu.SMEM),
+        out_shape=jax.ShapeDtypeStruct((owned, 1, kpoints, columns), jnp.float32),
+        in_specs=[pl.BlockSpec(memory_space=pl.ANY)] * 2
+        + [in_vmem] * 2
+        + [pl.BlockSpec(memory_space=pltpu.SMEM)] * 2,
+        out_specs=in_vmem,
+        scratch_shapes=[
+            pltpu.VMEM((radial, columns), jnp.bfloat16),
+            pltpu.VMEM((level_count, columns), jnp.float32),
+            pltpu.VMEM((slab_points, grid_count, columns), jnp.float32),
+            pltpu.VMEM((2, pieces, grid_count, share, slab_points, LANES), jnp.bfloat16),
+            pltpu.VMEM((wide[0][1] // LANES, rows, LANES), jnp.float32),
+            pltpu.VMEM((wide[1][1] // LANES, rows, LANES), jnp.float32),
+            pltpu.VMEM((level_count, total_j * slab_points, grid_count, columns), jnp.float32),
+            pltpu.VMEM((halves * ang_size,) + parts_shape, jnp.float32),
+            pltpu.VMEM((halves, chips) + parts_shape, jnp.float32),
+            pltpu.VMEM((halves, chips - 1) + parts_shape, jnp.float32),
+            pltpu.VMEM(slice_shape, jnp.float32),
+            pltpu.VMEM(slice_shape, jnp.float32),
+            pltpu.SemaphoreType.DMA((2, pieces)),
+            pltpu.SemaphoreType.DMA((2, halves, chips)),
+            pltpu.SemaphoreType.DMA((2, halves, chips)),
+            pltpu.SemaphoreType.DMA((2, halves, total_j)),
+            pltpu.SemaphoreType.DMA,
         ],
-        out_specs=pl.BlockSpec(memory_space=pltpu.VMEM),
-        scratch_shapes=[
-            pltpu.VMEM((2, pieces, grid_count, owned, slab_points, LANES), jnp.bfloat16),
-            pltpu.VMEM((2, rows, LANES), jnp.float32),
-            pltpu.VMEM((2, rows, LANES), jnp.float32),
-            pltpu.SemaphoreType.DMA((2, pieces)),
-        ],
-        compiler_params=pltpu.CompilerParams(vmem_limit_bytes=56 << 20),
+        compiler_params=pltpu.CompilerParams(
+            vmem_limit_bytes=56 << 20, collective_id=0, has_side_effects=True
+        ),
         name="block_kernel",
-    )(amplitude, ps_form, point_weights(sixj, projector, l_ps, qinverse), l_atom)
-    summed = lax.psum_scatter(partial, "ang", scatter_dimension=0, tiled=True)
-    summed = summed.reshape(owned, total_j, slab_points, columns)
-    return lax.all_to_all(summed, "kslab", split_axis=1, concat_axis=2, tiled=True)
+    )(
+        amplitude,
+        ps_form,
+        point_weights(sixj, projector),
+        l_ps.reshape(1, ps_channels),
+        kgrid,
+        l_atom,
+    )
 
 
 def solution(mesh):

time: 144 us -> 71.2 us (0.49)
  waiting for transfers between devices: 49.5 us -> 0 us
  blocking collectives: 16.3 us -> 0 us
  Pallas kernels: 50.4 us -> 66.6 us
  between operations: 13.5 us -> 0.05 us
  other arithmetic: 5.87 us -> 0.44 us
  matrix products: 3.46 us -> 0.25 us
    reduce_scatter x1 -> x0, waiting for transfers between devices: 49.5 us -> none  [local(): summed = lax.psum_scatter(partial, 'ang', scatter_dimension=0, tiled=True)]
    all_to_all x1 -> x0, blocking collectives: 16.3 us -> none  [local(): lax.all_to_all(summed, 'kslab', split_axis=1, concat_axis=2, tiled=True)]
    pallas_call x1, Pallas kernels: 50.4 us -> 66.6 us  [local(): pl.pallas_call(functools.partial(block_kernel, sizes), out_shape=jax.Shap...]
    mul x4 -> x1, other arithmetic: 3.92 us -> 0.05 us  [legendre_table(): grid_weights = jnp.pi / total_points * jnp.sin(angles)]
    dot_general x2 -> x0, matrix products: 3.46 us -> none  [the longest x1 3.2 us: point_weights(): jnp.einsum('xjgy,cy->xjgc', points, widened, precision=lax.Precision.HIGH...]
    unnamed x2 -> x3, local copies, waits for them, and re-layouts: 0.01 us -> 2.68 us
    reshape x3 -> x0, local copies, waits for them, and re-layouts: 1.51 us -> none  [the longest x2 1.28 us: local(): summed = summed.reshape(owned, total_j, slab_points, columns)]
  transfers between devices with their start and end apart: 1 -> 0, of which waited for: 1 -> 0; matrix products, arithmetic and copies ran while one was open for 0% -> 0% of each run, Pallas kernels for 0% -> 0%
where the time goes in v2:
time: 71.2 us; the launch traced here: 71 us
  Pallas kernels  66.6 us (94%)
  local copies, waits for them, and re-layouts  3.74 us (5%)
    pallas_call x1, Pallas kernels, local(): pl.pallas_call(functools.partial(block_kernel, sizes), out_shape=jax.Shap...  66.6 us
    unnamed x3, local copies, waits for them, and re-layouts  2.68 us

profile of v2, /device:TPU:0, one launch (start us, length us, event | category | flops | bytes accessed | tf_op | source)
XLA Modules:
  0.0 71.0 jit_solution(15667701737412405937)
XLA Ops:
  0.0 0.0 copy-start
  0.0 0.9 %copy-done = f32[4,12,8,8]{1,3,2,0:T(8,128)S(1)} copy-done((f32[4,12,8,8]{1,3,2,0:T(8,128)S(1)}, f32[4,12,8,8]{1,3,2,0:T(8,128)}, u32[]{:S(2)}) %copy-start) | copy-done | bytes 12312
  1.0 0.1 broadcast_multiply_fusion.3
  1.1 0.1 broadcast_multiply_fusion.5
  1.1 0.1 broadcast_multiply_fusion.1
  1.2 0.1 subtract_multiply_fusion
  1.3 0.1 multiply_cosine_fusion
  1.4 0.1 stack.2
  1.4 0.3 fusion
  1.7 1.0 %copy.7 = f32[8,4,32,8]{3,2,1,0:T(8,128)} copy(f32[8,4,32,8]{2,3,0,1:T(8,128)S(1)} %bitcast.11) | data formatting | bytes 65536 | tf_op jit(solution)/shard_map/jlxy,lg->xjgy/transpose | solution.py:344
  2.7 66.6 %block_kernel.1 = f32[14,1,8,896]{3,2,1,0:T(8,128)} custom-call(bf16[32,112,2,2048]{3,2,1,0:T(2,128)(2,1)} %amplitude.1, bf16[2048,896]{1,0:T(8,128)(2,1)} %ps_source.1, f32[8,128,8]{2,1,0:T(8,128)} %bitcast.10, s32[1,112]{1,0:T(1,128)} %bitcast.12, f32[8]{0:T(128)} %kgrid.1, s32[112]{0:T(128)} %levels.1), custom_call_target="tpu_custom_call" | custom-call | tf_op jit(solution)/shard_map/block_kernel/pallas_call | solution.py:373
  69.3 1.8 %copy.9 = f32[14,1,8,896]{3,2,1,0:T(8,128)} copy(f32[14,1,8,896]{3,2,1,0:T(8,128)} %block_kernel.1) | data formatting | bytes 802816
  (3 shorter events, 0.1 us)
Async XLA Ops:
  0.0 0.9 %copy-start = (f32[4,12,8,8]{1,3,2,0:T(8,128)S(1)}, f32[4,12,8,8]{1,3,2,0:T(8,128)}, u32[]{:S(2)}) copy-start(f32[4,12,8,8]{1,3,2,0:T(8,128)} %param.11) | copy-start | bytes 36868

commit v3 on v2

--- a/solution.py
+++ b/solution.py
@@ -65,6 +65,7 @@
 
 LANES = 128
 HALVES = 2
+SLOTS = 6
 
 
 def column_chunks(columns):
@@ -189,8 +190,14 @@
             device_id_type=pl.DeviceIdType.MESH,
         )
 
-    for copy in fetch(amplitude, slab, sems, 0, first_of(0), owned):
-        copy.start()
+    units = halves * blocks
+    slots = slab.shape[0]
+
+    def start_fetch(unit):
+        for copy in fetch(amplitude, slab, sems, lax.rem(unit, slots), first_of(unit), owned):
+            copy.start()
+
+    start_fetch(0)
     ps_copy = pltpu.make_async_copy(ps_source, ps_form, ps_sem)
     ps_copy.start()
     barrier = pltpu.get_barrier_semaphore()
@@ -201,7 +208,11 @@
         pl.semaphore_signal(
             barrier, inc=1, device_id=device, device_id_type=pl.DeviceIdType.MESH
         )
-    pl.semaphore_wait(barrier, len(greeted))
+    def start_early(unit, carry):
+        start_fetch(unit)
+        return carry
+
+    lax.fori_loop(1, min(slots - 1, units), start_early, 0)
 
     member = lax.broadcasted_iota(jnp.int32, (ps_levels.shape[1], columns), 1) - (
         kpoints * lax.broadcasted_iota(jnp.int32, (ps_levels.shape[1], columns), 0)
@@ -209,7 +220,8 @@
     member = jnp.where((member >= 0) & (member < kpoints), 1.0, 0.0).astype(jnp.bfloat16)
     level_rows = lax.broadcasted_iota(jnp.int32, (weights.shape[0], ps_levels.shape[1]), 0)
     known = jnp.where(level_rows == ps_levels[...], 1.0, 0.0).astype(jnp.bfloat16)
-    onehot[...] = jnp.dot(known, member, preferred_element_type=jnp.float32)
+    spread_rows = jnp.dot(known, member, preferred_element_type=jnp.float32)
+    onehot[...] = jnp.concatenate([spread_rows] * 3, axis=0).astype(jnp.bfloat16)
 
     tile_shape = (grid_count, LANES)
     place = me * grid_count + lax.broadcasted_iota(jnp.int32, tile_shape, 0)
@@ -225,21 +237,25 @@
         for tile in range(columns // LANES):
             qinverse[k, :, tile * LANES : (tile + 1) * LANES] = value
 
-    def weight_level(level, carry):
+    group = 4
+    level_size = total_j * grid_count
+    for first_level in range(0, weights.shape[0], group):
+        whole = points[first_level : first_level + group].reshape(group * level_size, -1)
+        high = whole.astype(jnp.bfloat16).astype(jnp.float32)
+        middle = (whole - high).astype(jnp.bfloat16).astype(jnp.float32)
+        low = whole - high - middle
         spread = jnp.dot(
-            points[level],
+            jnp.concatenate([high, middle, low], axis=1).astype(jnp.bfloat16),
             onehot[...],
-            precision=lax.Precision.HIGHEST,
             preferred_element_type=jnp.float32,
         )
-        for j in range(total_j):
+        for part in range(group * total_j):
+            rows_of = spread[part * grid_count : (part + 1) * grid_count]
             for k in range(slab_points):
-                weights[level, j * slab_points + k] = (
-                    spread[j * grid_count : (j + 1) * grid_count] * qinverse[k]
+                weights[first_level + part // total_j, part % total_j * slab_points + k] = (
+                    rows_of * qinverse[k]
                 )
-        return carry
-
-    lax.fori_loop(0, weights.shape[0], weight_level, 0)
+    pl.semaphore_wait(barrier, len(greeted))
     last_acc[...] = jnp.zeros_like(last_acc)
     ps_copy.wait()
 
@@ -295,14 +311,13 @@
                 slices_in[half, z] = slices[half, z]
 
     def step(unit, carry):
-        slot = lax.rem(unit, 2)
+        slot = lax.rem(unit, slots)
         for copy in fetch(amplitude, slab, sems, slot, first_of(unit), owned):
             copy.wait()
 
-        @pl.when(unit + 1 < halves * blocks)
+        @pl.when(unit + slots - 1 < units)
         def _():
-            for copy in fetch(amplitude, slab, sems, 1 - slot, first_of(unit + 1), owned):
-                copy.start()
+            start_fetch(unit + slots - 1)
 
         multiply(slot, 0)
         weigh_unit(jnp.maximum(unit - 1, 0), 1)
@@ -315,7 +330,6 @@
         weigh_unit(unit, 0)
         return carry
 
-    units = halves * blocks
     lax.fori_loop(0, units, step, 0)
     weigh_unit(units - 1, 1)
     finish(units - 1)
@@ -379,9 +393,9 @@
         out_specs=in_vmem,
         scratch_shapes=[
             pltpu.VMEM((radial, columns), jnp.bfloat16),
-            pltpu.VMEM((level_count, columns), jnp.float32),
+            pltpu.VMEM((3 * level_count, columns), jnp.bfloat16),
             pltpu.VMEM((slab_points, grid_count, columns), jnp.float32),
-            pltpu.VMEM((2, pieces, grid_count, share, slab_points, LANES), jnp.bfloat16),
+            pltpu.VMEM((SLOTS, pieces, grid_count, share, slab_points, LANES), jnp.bfloat16),
             pltpu.VMEM((wide[0][1] // LANES, rows, LANES), jnp.float32),
             pltpu.VMEM((wide[1][1] // LANES, rows, LANES), jnp.float32),
             pltpu.VMEM((level_count, total_j * slab_points, grid_count, columns), jnp.float32),
@@ -390,7 +404,7 @@
             pltpu.VMEM((halves, chips - 1) + parts_shape, jnp.float32),
             pltpu.VMEM(slice_shape, jnp.float32),
             pltpu.VMEM(slice_shape, jnp.float32),
-            pltpu.SemaphoreType.DMA((2, pieces)),
+            pltpu.SemaphoreType.DMA((SLOTS, pieces)),
             pltpu.SemaphoreType.DMA((2, halves, chips)),
             pltpu.SemaphoreType.DMA((2, halves, chips)),
             pltpu.SemaphoreType.DMA((2, halves, total_j)),

time: 71.2 us -> 70.4 us (0.989)
  Pallas kernels: 66.6 us -> 65.7 us
    pallas_call x1, Pallas kernels: 66.6 us -> 65.7 us  [local(): pl.pallas_call(functools.partial(block_kernel, sizes), out_shape=jax.Shap...]
where the time goes in v3:
time: 70.4 us; the launch traced here: 70.2 us
  Pallas kernels  65.7 us (93%)
  local copies, waits for them, and re-layouts  3.74 us (5%)
    pallas_call x1, Pallas kernels, local(): pl.pallas_call(functools.partial(block_kernel, sizes), out_shape=jax.Shap...  65.7 us
    unnamed x3, local copies, waits for them, and re-layouts  2.68 us

profile of v3, /device:TPU:0, one launch (start us, length us, event | category | flops | bytes accessed | tf_op | source)
XLA Modules:
  0.0 70.2 jit_solution(10931913815499918441)
XLA Ops:
  0.0 0.0 copy-start
  0.0 0.9 %copy-done = f32[4,12,8,8]{1,3,2,0:T(8,128)S(1)} copy-done((f32[4,12,8,8]{1,3,2,0:T(8,128)S(1)}, f32[4,12,8,8]{1,3,2,0:T(8,128)}, u32[]{:S(2)}) %copy-start) | copy-done | bytes 12312
  1.0 0.1 broadcast_multiply_fusion.3
  1.1 0.1 broadcast_multiply_fusion.5
  1.1 0.1 broadcast_multiply_fusion.1
  1.2 0.1 subtract_multiply_fusion
  1.3 0.1 multiply_cosine_fusion
  1.4 0.1 stack.2
  1.4 0.3 fusion
  1.7 1.0 %copy.7 = f32[8,4,32,8]{3,2,1,0:T(8,128)} copy(f32[8,4,32,8]{2,3,0,1:T(8,128)S(1)} %bitcast.11) | data formatting | bytes 65536 | tf_op jit(solution)/shard_map/jlxy,lg->xjgy/transpose | solution.py:358
  2.7 65.7 %block_kernel.1 = f32[14,1,8,896]{3,2,1,0:T(8,128)} custom-call(bf16[32,112,2,2048]{3,2,1,0:T(2,128)(2,1)} %amplitude.1, bf16[2048,896]{1,0:T(8,128)(2,1)} %ps_source.1, f32[8,128,8]{2,1,0:T(8,128)} %bitcast.10, s32[1,112]{1,0:T(1,128)} %bitcast.12, f32[8]{0:T(128)} %kgrid.1, s32[112]{0:T(128)} %levels.1), custom_call_target="tpu_custom_call" | custom-call | tf_op jit(solution)/shard_map/block_kernel/pallas_call | solution.py:387
  68.4 1.8 %copy.9 = f32[14,1,8,896]{3,2,1,0:T(8,128)} copy(f32[14,1,8,896]{3,2,1,0:T(8,128)} %block_kernel.1) | data formatting | bytes 802816
  (3 shorter events, 0.1 us)
Async XLA Ops:
  0.0 0.9 %copy-start = (f32[4,12,8,8]{1,3,2,0:T(8,128)S(1)}, f32[4,12,8,8]{1,3,2,0:T(8,128)}, u32[]{:S(2)}) copy-start(f32[4,12,8,8]{1,3,2,0:T(8,128)} %param.11) | copy-start | bytes 36868
